TPU v7x, 128 devices: a whole 4x4x4 slice. The times are simulated.
128 devices in a mesh: grp: 4 (over z), ep: 32 (over x, y, core).
Axes of the slice: x: 4, y: 4, z: 4, core: 2. Of those that a mesh axis runs over, the one named last changes fastest.
Arguments:
- attention: bfloat16 [16384, 1024], P(('grp', 'ep')), may hold values from -6 to 6
- residual: bfloat16 [16384, 1024], P(('grp', 'ep')), may hold values from -6 to 6
- out_proj: bfloat16 [1024, 1024], P(None, 'grp'), may hold values from -0.1875 to 0.1875
- pre_gain: float32 [1024], replicated, may hold values from 0.25 to 1.75
- post_gain: float32 [1024], replicated, may hold values from 0.25 to 1.75
- slot_gate_up: bfloat16 [32, 1024, 1024], P('ep'), may hold values from -0.1875 to 0.1875
- slot_down: bfloat16 [32, 512, 1024], P('ep'), may hold values from -0.25 to 0.25
- expert_ids: int32 [16384, 8], P(('grp', 'ep')), may hold values from 0 to 31, all different within a row
- copy_choice: int32 [16384, 8], P(('grp', 'ep')), may hold values from 0 to 3
- placement: int32 [32], replicated, may hold values from 0 to 31, each once
- request_age: int32 [16384], P(('grp', 'ep')), may hold values from 0 to 1048575
- decode_flag: int32 [16384], P(('grp', 'ep')), may hold values 0 or 1
- capacity: int32 [4, 32], replicated, may hold values from 4 to 8, as said below
- route_weight: float32 [16384, 8], P(('grp', 'ep')), may hold values from 0.05 to 1
Outputs:
- layer_out: bfloat16 [16384, 1024], P(('grp', 'ep'))
Inputs may be any that keep to these rules, and one draw needn't show every extreme that they name: At least one block has capacity 8. `expert_ids`: each row names 8 different experts. `placement`: each slot holds a different expert.
All inputs are finite; a program needn't handle non-finite values. No bound on the sum of `decode_flag` on one device may be relied on, other than what follows from the above.
Results may differ from a plain program's by a relative error of at most 0.01.
Values may be sent and summed in bfloat16 or wider, within the bound.
A program may use at most 64 MiB of HBM per device.

v0:
```python
import jax
import jax.numpy as jnp
from jax import lax
from jax.sharding import PartitionSpec as P


def rms_scale(values, gain):
    meansq = jnp.mean(values * values, axis=-1, keepdims=True)
    return values * lax.rsqrt(meansq + 1e-06) * gain


def on_device(
    attention,
    residual,
    out_proj,
    pre_gain,
    post_gain,
    slot_gate_up,
    slot_down,
    expert_ids,
    copy_choice,
    placement,
    request_age,
    decode_flag,
    capacity,
    route_weight,
):
    groups = lax.axis_size("grp")
    owners = lax.axis_size("ep")
    devices_all = groups * owners
    rows_here = attention.shape[0]
    features = attention.shape[1]
    picks_row = expert_ids.shape[1]
    cap_size = max(2, rows_here * picks_row // devices_all)
    columns = jnp.dot(
        lax.all_gather(attention, "grp", axis=0, tiled=True),
        out_proj,
        preferred_element_type=jnp.float32,
    )
    attn_proj = lax.all_to_all(columns, "grp", split_axis=0, concat_axis=1, tiled=True)
    hidden_state = (residual.astype(jnp.float32) + attn_proj).astype(jnp.bfloat16)
    normed = rms_scale(hidden_state.astype(jnp.float32), pre_gain).astype(jnp.bfloat16)
    experts_all = placement.shape[0]
    slot_table = jnp.arange(owners, dtype=jnp.int32)
    matches = (placement[None, :] == jnp.arange(experts_all, dtype=jnp.int32)[:, None]).astype(
        jnp.int32
    )
    slot_of = jnp.sum(slot_table[None, :] * matches, axis=1)
    expert_hits = (
        expert_ids[:, :, None] == jnp.arange(experts_all, dtype=jnp.int32)[None, None, :]
    ).astype(jnp.int32)
    target = copy_choice * owners + jnp.sum(expert_hits * slot_of[None, None, :], axis=2)
    priority = decode_flag * 1048576 + request_age
    order = jnp.arange(rows_here, dtype=jnp.int32)
    ahead_mask = (priority[None, :] > priority[:, None]) | (
        priority[None, :] == priority[:, None]
    ) & (order[None, :] < order[:, None])
    target_hits = jnp.sum(
        (target[:, :, None] == jnp.arange(devices_all, dtype=jnp.int32)[None, None, :]).astype(
            jnp.bfloat16
        ),
        axis=1,
    )
    counts = jnp.dot(
        ahead_mask.astype(jnp.bfloat16), target_hits, preferred_element_type=jnp.float32
    )
    position = jnp.take_along_axis(counts, target, axis=1).astype(jnp.int32)
    granted = jnp.take(capacity.reshape(-1), target)
    accepted = position < granted
    total_slots = devices_all * cap_size
    index = jnp.where(accepted, target * cap_size + position, total_slots)
    spread_rows = jnp.broadcast_to(normed[:, None, :], (rows_here, picks_row, features)).reshape(
        rows_here * picks_row, features
    )
    buffer = (
        jnp.zeros((total_slots, features), jnp.bfloat16)
        .at[index.reshape(-1)]
        .set(spread_rows, mode="drop")
    )
    gate_up_local = slot_gate_up[0]
    down_local = slot_down[0]
    hidden_units = down_local.shape[0]
    arrived = lax.all_to_all(
        buffer.reshape(devices_all, cap_size, features),
        ("grp", "ep"),
        split_axis=0,
        concat_axis=0,
        tiled=True,
    )
    flattened = arrived.reshape(-1, features)
    gate_up = jnp.dot(flattened, gate_up_local, preferred_element_type=jnp.float32)
    expert_hidden = (jax.nn.silu(gate_up[:, :hidden_units]) * gate_up[:, hidden_units:]).astype(
        jnp.bfloat16
    )
    produced = jnp.dot(expert_hidden, down_local, preferred_element_type=jnp.float32).astype(
        jnp.bfloat16
    )
    returned = lax.all_to_all(
        produced.reshape(arrived.shape), ("grp", "ep"), split_axis=0, concat_axis=0, tiled=True
    )
    flat_back = returned.reshape(total_slots, features)
    expert_out = flat_back[jnp.minimum(index, total_slots - 1)]
    weights_kept = jnp.where(accepted, route_weight, jnp.float32(0.0))
    mixture = jnp.einsum("rk,rkd->rd", weights_kept, expert_out, preferred_element_type=jnp.float32)
    return rms_scale(hidden_state.astype(jnp.float32) + mixture, post_gain).astype(jnp.bfloat16)


def solution(mesh):
    placed = (
        P(("grp", "ep"), None),
        P(("grp", "ep"), None),
        P(None, "grp"),
        P(),
        P(),
        P("ep", None, None),
        P("ep", None, None),
        P(("grp", "ep"), None),
        P(("grp", "ep"), None),
        P(),
        P(("grp", "ep")),
        P(("grp", "ep")),
        P(),
        P(("grp", "ep"), None),
    )
    return jax.shard_map(
        on_device, mesh=mesh, in_specs=placed, out_specs=P(("grp", "ep"), None), check_vma=False
    )
```

profile of v0, /device:TPU:1, one launch (start us, length us, event | category | flops | bytes accessed | tf_op | source)
XLA Modules:
  0.0 155.6 jit_solution(14246727109927637221)
XLA Ops:
  6.5 0.7 all-gather.2.cloned.1.call-update
  7.3 0.8 select_reduce_fusion.1
  8.0 0.8 select_reduce_fusion
  8.8 0.7 bitcast_or_fusion
  9.8 0.2 fusion.17
  10.1 0.7 multiply_add_fusion.1
  10.7 0.2 fusion.20
  10.9 6.8 %gather_fusion.2 = f32[1024]{0:T(1024)S(1)} fusion(f32[128,128]{1,0:T(8,128)S(1)} %fusion.20, s32[1024]{0:T(1024)S(1)} %reshape.110), kind=kCustom, calls=%fused_computation.2 | custom fusion | bytes 16384 | tf_op jit(solution)/shard_map/jit(take_along_axis)/gather | solution.py:67
  18.2 6.6 %gather_fusion = s32[1024]{0:T(1024)S(1)} fusion(s32[128]{0:T(128)S(1)} %reshape.87, s32[1024]{0:T(1024)S(1)} %broadcast_clamp_fusion.1), kind=kCustom, calls=%fused_computation | custom fusion | bytes 12288 | tf_op jit(solution)/shard_map/jit(_take)/gather | solution.py:68
  24.9 10.7 %all-gather.2.cloned.1.call-done = bf16[512,1024]{1,0:T(8,128)(2,1)} async-done(((bf16[128,1024]{1,0:T(8,128)(2,1)}), bf16[512,1024]{1,0:T(8,128)(2,1)}) %all-gather.2.cloned.1.call-update) | async-done | bytes 1048592 | tf_op jit(solution)/shard_map/all_gather | solution.py:36
  35.6 2.5 %fusion.27 = f32[512,256]{1,0:T(8,128)} fusion(bf16[512,1024]{1,0:T(8,128)(2,1)} %all-gather.2.cloned.1.call-done, bf16[1024,256]{1,0:T(8,128)(2,1)S(1)} %copy-done.1), kind=kOutput, calls=%fused_computation.57 | convolution fusion | flops 268435456 | bytes 2097152 | tf_op jit(solution)/shard_map/dot_general | solution.py:35
  38.1 3.6 %all-to-all-start = ((f32[4,128,256]{2,1,0:T(8,128)}), f32[4,128,256]{2,1,0:T(8,128)S(1)}, u32[]{:S(2)}, u32[]{:S(2)}) async-start(f32[4,128,256]{2,1,0:T(8,128)} %bitcast), calls=%async_computation | async-start | bytes 1048576 | tf_op jit(solution)/shard_map/all_to_all | solution.py:40
  41.9 7.3 %all-to-all-done = f32[4,128,256]{2,1,0:T(8,128)S(1)} async-done(((f32[4,128,256]{2,1,0:T(8,128)}), f32[4,128,256]{2,1,0:T(8,128)S(1)}, u32[]{:S(2)}, u32[]{:S(2)}) %all-to-all-start) | async-done | bytes 524320 | tf_op jit(solution)/shard_map/all_to_all | solution.py:40
  49.2 0.2 fusion.13
  49.6 6.8 %scatter_custom_fusion = bf16[1024,1024]{1,0:T(8,128)(2,1)} fusion(s32[1024]{0:T(1024)S(1)} %bitcast.43, bf16[128,1024]{1,0:T(8,128)(2,1)S(1)} %fusion.15, bf16[]{:T(256)} %constant.29.clone.1), kind=kCustom, calls=%fused_computation.11 | custom fusion | bytes 2359298 | tf_op jit(solution)/shard_map/scatter | solution.py:78
  56.4 40.3 %all_to_all.29 = bf16[128,8,1024]{2,1,0:T(8,128)(2,1)S(1)} all-to-all(bf16[128,8,1024]{2,1,0:T(8,128)(2,1)} %bitcast.40), channel_id=1, replica_groups=mesh['grp'=4,'ep'=32] {'grp','ep'}, dimensions={0} | all-to-all | bytes 4194304 | tf_op jit(solution)/shard_map/all_to_all | solution.py:83
  96.7 2.4 %fusion.3 = f32[1024,1024]{1,0:T(8,128)S(1)} fusion(bf16[1,1024,1024]{2,1,0:T(8,128)(2,1)S(1)} %copy-done, bf16[128,8,1024]{2,1,0:T(8,128)(2,1)S(1)} %all_to_all.29), kind=kOutput, calls=%fused_computation.8 | convolution fusion | flops 2147483648 | bytes 8388608 | tf_op jit(solution)/shard_map/dot_general | solution.py:91
  99.1 2.6 %convert_bitcast_fusion = bf16[128,8,1024]{2,1,0:T(8,128)(2,1)} fusion(f32[1024,1024]{1,0:T(8,128)S(1)} %fusion.3, bf16[1,512,1024]{2,1,0:T(8,128)(2,1)S(1)} %copy-done.7), kind=kOutput, calls=%fused_computation.13 | convolution fusion | flops 1077936128 | bytes 7340032 | tf_op jit(solution)/shard_map/dot_general | solution.py:95
  101.7 5.5 %all-to-all-start.2 = ((bf16[128,8,1024]{2,1,0:T(8,128)(2,1)}), bf16[128,8,1024]{2,1,0:T(8,128)(2,1)}, u32[]{:S(2)}, u32[]{:S(2)}) async-start(bf16[128,8,1024]{2,1,0:T(8,128)(2,1)} %convert_bitcast_fusion), calls=%async_computation.2 | async-start | bytes 4194304 | tf_op jit(solution)/shard_map/all_to_all | solution.py:98
  107.6 29.9 %all-to-all-done.2 = bf16[128,8,1024]{2,1,0:T(8,128)(2,1)} async-done(((bf16[128,8,1024]{2,1,0:T(8,128)(2,1)}), bf16[128,8,1024]{2,1,0:T(8,128)(2,1)}, u32[]{:S(2)}, u32[]{:S(2)}) %all-to-all-start.2) | async-done | bytes 2097184 | tf_op jit(solution)/shard_map/all_to_all | solution.py:98
  137.5 7.9 %gather_fusion.1 = bf16[1024,1024]{1,0:T(8,128)(2,1)} fusion(bf16[1024,1024]{1,0:T(8,128)(2,1)} %bitcast.11, s32[1024]{0:T(1024)S(1)} %broadcast_clamp_fusion), kind=kCustom, calls=%fused_computation.1 | custom fusion | bytes 4198400 | tf_op jit(solution)/shard_map/gather | solution.py:102
  145.5 2.3 %fusion.1 = f32[128,1,1024]{2,1,0:T(1,128)S(1)} fusion(bf16[128,8,1]{1,2,0:T(2,128)(2,1)S(1)} %copy.31, bf16[1024,1024]{1,0:T(8,128)(2,1)} %gather_fusion.1), kind=kOutput, calls=%fused_computation.6 | convolution fusion | flops 2097152 | bytes 2623488 | tf_op jit(solution)/shard_map/rk,rkd->rd/dot_general | solution.py:104
  147.8 0.2 multiply_reduce_fusion
  147.9 0.8 multiply_convert_fusion
  (42 shorter events, 1.6 us)
Async XLA Ops:
  6.5 90.2 %copy-start = (bf16[1,1024,1024]{2,1,0:T(8,128)(2,1)S(1)}, bf16[1,1024,1024]{2,1,0:T(8,128)(2,1)}, u32[]{:S(2)}) copy-start(bf16[1,1024,1024]{2,1,0:T(8,128)(2,1)} %param.19) | copy-start | bytes 6291460
  6.5 29.1 %all-gather.2.cloned.1.call-start = ((), (), s32[]{:S(2)}) async-start(), calls=%async_computation.3 | async-start | bytes 1310720 | tf_op jit(solution)/shard_map/all_gather | solution.py:36
  10.9 7.2 %copy-start.6 = (s32[4,32]{1,0:T(4,128)S(1)}, s32[4,32]{1,0:T(4,128)}, u32[]{:S(2)}) copy-start(s32[4,32]{1,0:T(4,128)} %param.26) | copy-start | bytes 1540
  18.2 17.4 %copy-start.1 = (bf16[1024,256]{1,0:T(8,128)(2,1)S(1)}, bf16[1024,256]{1,0:T(8,128)(2,1)}, u32[]{:S(2)}) copy-start(bf16[1024,256]{1,0:T(8,128)(2,1)} %param.16) | copy-start | bytes 1572868
  24.9 24.3 %copy-start.2 = (bf16[128,1024]{1,0:T(8,128)(2,1)S(1)}, bf16[128,1024]{1,0:T(8,128)(2,1)}, u32[]{:S(2)}) copy-start(bf16[128,1024]{1,0:T(8,128)(2,1)} %param.15) | copy-start | bytes 786436
  38.1 11.3 %copy-start.3 = (f32[1024]{0:T(1024)S(1)}, f32[1024]{0:T(1024)}, u32[]{:S(2)}) copy-start(f32[1024]{0:T(1024)} %param.17) | copy-start | bytes 12292
  38.1 11.1 %all-to-all-start = ((f32[4,128,256]{2,1,0:T(8,128)}), f32[4,128,256]{2,1,0:T(8,128)S(1)}, u32[]{:S(2)}, u32[]{:S(2)}) async-start(f32[4,128,256]{2,1,0:T(8,128)} %bitcast), calls=%async_computation | async-start | bytes 1048576 | tf_op jit(solution)/shard_map/all_to_all | solution.py:40
  96.7 2.4 %copy-start.7 = (bf16[1,512,1024]{2,1,0:T(8,128)(2,1)S(1)}, bf16[1,512,1024]{2,1,0:T(8,128)(2,1)}, u32[]{:S(2)}) copy-start(bf16[1,512,1024]{2,1,0:T(8,128)(2,1)} %param.20) | copy-start | bytes 3145732
  101.7 5.7 %copy-start.5 = (f32[128,8]{0,1:T(8,128)S(1)}, f32[128,8]{0,1:T(8,128)}, u32[]{:S(2)}) copy-start(f32[128,8]{0,1:T(8,128)} %param.27) | copy-start | bytes 12292
  101.7 35.9 %all-to-all-start.2 = ((bf16[128,8,1024]{2,1,0:T(8,128)(2,1)}), bf16[128,8,1024]{2,1,0:T(8,128)(2,1)}, u32[]{:S(2)}, u32[]{:S(2)}) async-start(bf16[128,8,1024]{2,1,0:T(8,128)(2,1)} %convert_bitcast_fusion), calls=%async_computation.2 | async-start | bytes 4194304 | tf_op jit(solution)/shard_map/all_to_all | solution.py:98
  145.5 2.5 %copy-start.4 = (f32[1024]{0:T(1024)S(1)}, f32[1024]{0:T(1024)}, u32[]{:S(2)}) copy-start(f32[1024]{0:T(1024)} %param.18) | copy-start | bytes 12292
Sparse Core Ops, SparseCore 0:
  9.0 26.5 all-gather.1
where the time goes:
time: 156 us
  waiting for transfers between devices  48.6 us (31%)
  blocking collectives  40.3 us (26%)
  local copies, waits for them, and re-layouts  29.5 us (19%)
  between operations  13.6 us (9%)
  matrix products  9.91 us (6%)
  starting transfers between devices  9.14 us (6%)
  other arithmetic  4.53 us (3%)
    all_to_all x1, blocking collectives, on_device(): lax.all_to_all(buffer.reshape(devices_all, cap_size, features), ('grp', '...  40.3 us
    all_to_all x1, waiting for transfers between devices, on_device(): lax.all_to_all(produced.reshape(arrived.shape), ('grp', 'ep'), split_axis...  29.9 us
    all_gather x1, waiting for transfers between devices, on_device(): lax.all_gather(attention, 'grp', axis=0, tiled=True)  10.7 us
    gather x1, local copies, waits for them, and re-layouts, on_device(): expert_out = flat_back[jnp.minimum(index, total_slots - 1)]  7.92 us
    all_to_all x1, waiting for transfers between devices, on_device(): lax.all_to_all(columns, 'grp', split_axis=0, concat_axis=1, tiled=True)  7.26 us
    gather x5, local copies, waits for them, and re-layouts, on_device(): position = jnp.take_along_axis(counts, target, axis=1).astype(jnp.int32)  7.12 us
    scatter x1, local copies, waits for them, and re-layouts, on_device(): buffer = jnp.zeros((total_slots, features), jnp.bfloat16).at[index.reshap...  6.83 us
    gather x3, local copies, waits for them, and re-layouts, on_device(): granted = jnp.take(capacity.reshape(-1), target)  6.7 us
  transfers between devices with their start and end apart: 3, of which 3 were waited for; matrix products, arithmetic and copies ran while one was open for 12% of the time, Pallas kernels for 0%

commit v1 on v0

--- a/solution.py
+++ b/solution.py
@@ -2,6 +2,18 @@
 import jax.numpy as jnp
 from jax import lax
 from jax.sharding import PartitionSpec as P
+
+
+def doubled_up(value, axis, dim):
+    ways, here, step = (lax.axis_size(axis), lax.axis_index(axis), value.shape[dim])
+    line, have = (value, 1)
+    while have < ways:
+        line = jnp.concatenate(
+            [line, lax.ppermute(line, axis, [(d, (d - have) % ways) for d in range(ways)])],
+            axis=dim,
+        )
+        have = 2 * have
+    return jnp.roll(line, here * step, axis=dim)
 
 
 def rms_scale(values, gain):
@@ -32,11 +44,7 @@
     features = attention.shape[1]
     picks_row = expert_ids.shape[1]
     cap_size = max(2, rows_here * picks_row // devices_all)
-    columns = jnp.dot(
-        lax.all_gather(attention, "grp", axis=0, tiled=True),
-        out_proj,
-        preferred_element_type=jnp.float32,
-    )
+    columns = jnp.dot(doubled_up(attention, "grp", 0), out_proj, preferred_element_type=jnp.float32)
     attn_proj = lax.all_to_all(columns, "grp", split_axis=0, concat_axis=1, tiled=True)
     hidden_state = (residual.astype(jnp.float32) + attn_proj).astype(jnp.bfloat16)
     normed = rms_scale(hidden_state.astype(jnp.float32), pre_gain).astype(jnp.bfloat16)

time: 156 us -> 142 us (0.910)
  between operations: 13.6 us -> 0.24 us
  waiting for transfers between devices: 48.6 us -> 38.8 us
  starting transfers between devices: 9.14 us -> 15.6 us
  other arithmetic: 4.53 us -> 6.29 us
    all_gather x1 -> x0, waiting for transfers between devices: 10.7 us -> none  [on_device(): lax.all_gather(attention, 'grp', axis=0, tiled=True)]
    ppermute x0 -> x2, starting transfers between devices: none -> 6.52 us  [doubled_up(): lax.ppermute(line, axis, [(d, (d - have) % ways) for d in range(ways)])]
    ppermute x0 -> x2, waiting for transfers between devices: none -> 1.81 us  [doubled_up(): lax.ppermute(line, axis, [(d, (d - have) % ways) for d in range(ways)])]
    concatenate x0 -> x1, other arithmetic: none -> 1.76 us  [doubled_up(): jnp.concatenate([line, lax.ppermute(line, axis, [(d, (d - have) % ways) f...]
  transfers between devices with their start and end apart: 3 -> 4, of which waited for: 3 -> 3; matrix products, arithmetic and copies ran while one was open for 12% -> 13% of each run, Pallas kernels for 0% -> 0%
where the time goes in v1:
time: 142 us; the launch traced here: 141 us
  blocking collectives  41.2 us (29%)
  waiting for transfers between devices  38.8 us (27%)
  local copies, waits for them, and re-layouts  30.6 us (22%)
  starting transfers between devices  15.6 us (11%)
  matrix products  8.68 us (6%)
  other arithmetic  6.29 us (4%)
    all_to_all x1, blocking collectives, on_device(): lax.all_to_all(buffer.reshape(devices_all, cap_size, features), ('grp', '...  41.2 us
    all_to_all x1, waiting for transfers between devices, on_device(): lax.all_to_all(produced.reshape(arrived.shape), ('grp', 'ep'), split_axis...  29.9 us
    gather x1, local copies, waits for them, and re-layouts, on_device(): expert_out = flat_back[jnp.minimum(index, total_slots - 1)]  7.92 us
    gather x5, local copies, waits for them, and re-layouts, on_device(): position = jnp.take_along_axis(counts, target, axis=1).astype(jnp.int32)  7.12 us
    all_to_all x1, waiting for transfers between devices, on_device(): lax.all_to_all(columns, 'grp', split_axis=0, concat_axis=1, tiled=True)  7.06 us
    scatter x1, local copies, waits for them, and re-layouts, on_device(): buffer = jnp.zeros((total_slots, features), jnp.bfloat16).at[index.reshap...  6.83 us
    gather x3, local copies, waits for them, and re-layouts, on_device(): granted = jnp.take(capacity.reshape(-1), target)  6.7 us
    ppermute x2, starting transfers between devices, doubled_up(): lax.ppermute(line, axis, [(d, (d - have) % ways) for d in range(ways)])  6.52 us
  transfers between devices with their start and end apart: 4, of which 3 were waited for; matrix products, arithmetic and copies ran while one was open for 13% of the time, Pallas kernels for 0%

profile of v1, /device:TPU:1, one launch (start us, length us, event | category | flops | bytes accessed | tf_op | source)
XLA Modules:
  0.0 141.5 jit_solution(15915962606849869417)
XLA Ops:
  0.0 4.6 %collective-permute-start = (bf16[128,1024]{1,0:T(8,128)(2,1)}, bf16[128,1024]{1,0:T(8,128)(2,1)S(1)}, u32[]{:S(2)}, u32[]{:S(2)}) collective-permute-start(bf16[128,1024]{1,0:T(8,128)(2,1)} %param.14), channel_id=1, source_target_pairs={{0,96},{32,0},{64,32},{96,64},{1,97},{33,1},{65,33},{97,65},{2,98}... | collective-permute-start | bytes 786440 | tf_op jit(solution)/shard_map/ppermute | solution.py:12
  4.6 0.8 select_reduce_fusion.1
  5.4 0.8 select_reduce_fusion
  6.1 0.7 bitcast_or_fusion
  6.9 0.7 multiply_add_fusion.1
  7.6 0.2 fusion.19
  8.1 1.8 %collective-permute-done = bf16[128,1024]{1,0:T(8,128)(2,1)S(1)} collective-permute-done((bf16[128,1024]{1,0:T(8,128)(2,1)}, bf16[128,1024]{1,0:T(8,128)(2,1)S(1)}, u32[]{:S(2)}, u32[]{:S(2)}) %collective-permute-start) | collective-permute-done | bytes 262176 | tf_op jit(solution)/shard_map/ppermute | solution.py:12
  9.9 1.8 %pad_maximum_fusion = bf16[256,1024]{1,0:T(8,128)(2,1)} fusion(bf16[128,1024]{1,0:T(8,128)(2,1)S(1)} %collective-permute-done, bf16[128,1024]{1,0:T(8,128)(2,1)} %param.14), kind=kLoop, calls=%fused_computation.26 | loop fusion | flops 1048576 | bytes 1048576 | tf_op jit(solution)/shard_map/concatenate | solution.py:11
  11.6 1.9 %collective-permute-start.1 = (bf16[256,1024]{1,0:T(8,128)(2,1)}, bf16[256,1024]{1,0:T(8,128)(2,1)S(1)}, u32[]{:S(2)}, u32[]{:S(2)}) collective-permute-start(bf16[256,1024]{1,0:T(8,128)(2,1)} %pad_maximum_fusion), channel_id=1, source_target_pairs={{0,64},{32,96},{64,0},{96,32},{1,65},{33,97},{65,1},{97,33},{2,66}... | collective-permute-start | bytes 1572872 | tf_op jit(solution)/shard_map/ppermute | solution.py:12
  13.8 6.8 %gather_fusion.2 = f32[1024]{0:T(1024)S(1)} fusion(f32[128,128]{1,0:T(8,128)S(1)} %fusion.22, s32[1024]{0:T(1024)S(1)} %reshape.110), kind=kCustom, calls=%fused_computation.2 | custom fusion | bytes 16384 | tf_op jit(solution)/shard_map/jit(take_along_axis)/gather | solution.py:75
  21.0 6.6 %gather_fusion = s32[1024]{0:T(1024)S(1)} fusion(s32[128]{0:T(128)S(1)} %reshape.87, s32[1024]{0:T(1024)S(1)} %broadcast_clamp_fusion.1), kind=kCustom, calls=%fused_computation | custom fusion | bytes 12288 | tf_op jit(solution)/shard_map/jit(_take)/gather | solution.py:76
  28.0 0.8 copy-done.2
  28.8 1.2 fusion.13
  30.0 3.6 %all-to-all-start = ((f32[4,128,256]{2,1,0:T(8,128)}), f32[4,128,256]{2,1,0:T(8,128)S(1)}, u32[]{:S(2)}, u32[]{:S(2)}) async-start(f32[4,128,256]{2,1,0:T(8,128)} %bitcast), calls=%async_computation | async-start | bytes 1048576 | tf_op jit(solution)/shard_map/all_to_all | solution.py:48
  33.9 7.1 %all-to-all-done = f32[4,128,256]{2,1,0:T(8,128)S(1)} async-done(((f32[4,128,256]{2,1,0:T(8,128)}), f32[4,128,256]{2,1,0:T(8,128)S(1)}, u32[]{:S(2)}, u32[]{:S(2)}) %all-to-all-start) | async-done | bytes 524320 | tf_op jit(solution)/shard_map/all_to_all | solution.py:48
  41.3 6.8 %scatter_custom_fusion = bf16[1024,1024]{1,0:T(8,128)(2,1)} fusion(s32[1024]{0:T(1024)S(1)} %bitcast.42, bf16[128,1024]{1,0:T(8,128)(2,1)S(1)} %fusion.17, bf16[]{:T(256)} %constant.78.clone.1), kind=kCustom, calls=%fused_computation.11 | custom fusion | bytes 2359298 | tf_op jit(solution)/shard_map/scatter | solution.py:86
  48.2 41.2 %all_to_all.29 = bf16[128,8,1024]{2,1,0:T(8,128)(2,1)S(1)} all-to-all(bf16[128,8,1024]{2,1,0:T(8,128)(2,1)} %bitcast.39), channel_id=1, replica_groups=mesh['grp'=4,'ep'=32] {'grp','ep'}, dimensions={0} | all-to-all | bytes 4194304 | tf_op jit(solution)/shard_map/all_to_all | solution.py:91
  89.4 2.4 %fusion.3 = f32[1024,1024]{1,0:T(8,128)S(1)} fusion(bf16[1,1024,1024]{2,1,0:T(8,128)(2,1)S(1)} %copy-done, bf16[128,8,1024]{2,1,0:T(8,128)(2,1)S(1)} %all_to_all.29), kind=kOutput, calls=%fused_computation.8 | convolution fusion | flops 2147483648 | bytes 8388608 | tf_op jit(solution)/shard_map/dot_general | solution.py:99
  91.8 2.6 %convert_bitcast_fusion = bf16[128,8,1024]{2,1,0:T(8,128)(2,1)} fusion(f32[1024,1024]{1,0:T(8,128)S(1)} %fusion.3, bf16[1,512,1024]{2,1,0:T(8,128)(2,1)S(1)} %copy-done.8), kind=kOutput, calls=%fused_computation.13 | convolution fusion | flops 1077936128 | bytes 7340032 | tf_op jit(solution)/shard_map/dot_general | solution.py:103
  94.4 5.5 %all-to-all-start.2 = ((bf16[128,8,1024]{2,1,0:T(8,128)(2,1)}), bf16[128,8,1024]{2,1,0:T(8,128)(2,1)}, u32[]{:S(2)}, u32[]{:S(2)}) async-start(bf16[128,8,1024]{2,1,0:T(8,128)(2,1)} %convert_bitcast_fusion), calls=%async_computation.2 | async-start | bytes 4194304 | tf_op jit(solution)/shard_map/all_to_all | solution.py:106
  100.3 29.9 %all-to-all-done.2 = bf16[128,8,1024]{2,1,0:T(8,128)(2,1)} async-done(((bf16[128,8,1024]{2,1,0:T(8,128)(2,1)}), bf16[128,8,1024]{2,1,0:T(8,128)(2,1)}, u32[]{:S(2)}, u32[]{:S(2)}) %all-to-all-start.2) | async-done | bytes 2097184 | tf_op jit(solution)/shard_map/all_to_all | solution.py:106
  130.2 7.9 %gather_fusion.1 = bf16[1024,1024]{1,0:T(8,128)(2,1)} fusion(bf16[1024,1024]{1,0:T(8,128)(2,1)} %bitcast.11, s32[1024]{0:T(1024)S(1)} %broadcast_clamp_fusion), kind=kCustom, calls=%fused_computation.1 | custom fusion | bytes 4198400 | tf_op jit(solution)/shard_map/gather | solution.py:110
  138.2 2.3 %fusion.1 = f32[128,1,1024]{2,1,0:T(1,128)S(1)} fusion(bf16[128,8,1]{1,2,0:T(2,128)(2,1)S(1)} %copy.31, bf16[1024,1024]{1,0:T(8,128)(2,1)} %gather_fusion.1), kind=kOutput, calls=%fused_computation.6 | convolution fusion | flops 2097152 | bytes 2623488 | tf_op jit(solution)/shard_map/rk,rkd->rd/dot_general | solution.py:112
  140.6 0.8 multiply_convert_fusion
  (52 shorter events, 2.3 us)
Async XLA Ops:
  0.0 89.4 %copy-start = (bf16[1,1024,1024]{2,1,0:T(8,128)(2,1)S(1)}, bf16[1,1024,1024]{2,1,0:T(8,128)(2,1)}, u32[]{:S(2)}) copy-start(bf16[1,1024,1024]{2,1,0:T(8,128)(2,1)} %param.19) | copy-start | bytes 6291460
  0.0 9.9 %collective-permute-start = (bf16[128,1024]{1,0:T(8,128)(2,1)}, bf16[128,1024]{1,0:T(8,128)(2,1)S(1)}, u32[]{:S(2)}, u32[]{:S(2)}) collective-permute-start(bf16[128,1024]{1,0:T(8,128)(2,1)} %param.14), channel_id=1, source_target_pairs={{0,96},{32,0},{64,32},{96,64},{1,97},{33,1},{65,33},{97,65},{2,98}... | collective-permute-start | bytes 786440 | tf_op jit(solution)/shard_map/ppermute | solution.py:12
  11.6 16.2 %collective-permute-start.1 = (bf16[256,1024]{1,0:T(8,128)(2,1)}, bf16[256,1024]{1,0:T(8,128)(2,1)S(1)}, u32[]{:S(2)}, u32[]{:S(2)}) collective-permute-start(bf16[256,1024]{1,0:T(8,128)(2,1)} %pad_maximum_fusion), channel_id=1, source_target_pairs={{0,64},{32,96},{64,0},{96,32},{1,65},{33,97},{65,1},{97,33},{2,66}... | collective-permute-start | bytes 1572872 | tf_op jit(solution)/shard_map/ppermute | solution.py:12
  13.8 7.2 %copy-start.7 = (s32[4,32]{1,0:T(4,128)S(1)}, s32[4,32]{1,0:T(4,128)}, u32[]{:S(2)}) copy-start(s32[4,32]{1,0:T(4,128)} %param.26) | copy-start | bytes 1540
  21.0 6.7 %copy-start.1 = (bf16[128,1024]{1,0:T(8,128)(2,1)S(1)}, bf16[128,1024]{1,0:T(8,128)(2,1)}, u32[]{:S(2)}) copy-start(bf16[128,1024]{1,0:T(8,128)(2,1)} %param.14) | copy-start | bytes 786436
  27.8 1.1 copy-start.2
  28.8 12.2 %copy-start.3 = (bf16[128,1024]{1,0:T(8,128)(2,1)S(1)}, bf16[128,1024]{1,0:T(8,128)(2,1)}, u32[]{:S(2)}) copy-start(bf16[128,1024]{1,0:T(8,128)(2,1)} %param.15) | copy-start | bytes 786436
  30.0 11.1 %copy-start.4 = (f32[1024]{0:T(1024)S(1)}, f32[1024]{0:T(1024)}, u32[]{:S(2)}) copy-start(f32[1024]{0:T(1024)} %param.17) | copy-start | bytes 12292
  30.0 10.9 %all-to-all-start = ((f32[4,128,256]{2,1,0:T(8,128)}), f32[4,128,256]{2,1,0:T(8,128)S(1)}, u32[]{:S(2)}, u32[]{:S(2)}) async-start(f32[4,128,256]{2,1,0:T(8,128)} %bitcast), calls=%async_computation | async-start | bytes 1048576 | tf_op jit(solution)/shard_map/all_to_all | solution.py:48
  89.4 2.4 %copy-start.8 = (bf16[1,512,1024]{2,1,0:T(8,128)(2,1)S(1)}, bf16[1,512,1024]{2,1,0:T(8,128)(2,1)}, u32[]{:S(2)}) copy-start(bf16[1,512,1024]{2,1,0:T(8,128)(2,1)} %param.20) | copy-start | bytes 3145732
  94.4 5.7 %copy-start.6 = (f32[128,8]{0,1:T(8,128)S(1)}, f32[128,8]{0,1:T(8,128)}, u32[]{:S(2)}) copy-start(f32[128,8]{0,1:T(8,128)} %param.27) | copy-start | bytes 12292
  94.4 35.8 %all-to-all-start.2 = ((bf16[128,8,1024]{2,1,0:T(8,128)(2,1)}), bf16[128,8,1024]{2,1,0:T(8,128)(2,1)}, u32[]{:S(2)}, u32[]{:S(2)}) async-start(bf16[128,8,1024]{2,1,0:T(8,128)(2,1)} %convert_bitcast_fusion), calls=%async_computation.2 | async-start | bytes 4194304 | tf_op jit(solution)/shard_map/all_to_all | solution.py:106
  138.2 2.5 %copy-start.5 = (f32[1024]{0:T(1024)S(1)}, f32[1024]{0:T(1024)}, u32[]{:S(2)}) copy-start(f32[1024]{0:T(1024)} %param.18) | copy-start | bytes 12292
